TPU v7x, 32 devices: a whole 2x2x4 slice. The times are simulated.
32 devices in a mesh: grp: 2 (over y), lat: 4 (over z), lon: 2 (over x), lev: 2 (over core).
Axes of the slice: x: 2, y: 2, z: 4, core: 2. Of those that a mesh axis runs over, the one named last changes fastest.
Arguments:
- snapshot: bfloat16 [256, 128, 512], P(('grp', 'lev'), 'lat', 'lon'), parts along dimension 0, may hold values from -6 to 6
- level_factor: bfloat16 [128, 48], P('lev'), may hold values from -0.75 to 0.75
- lon_factor: bfloat16 [512, 192], P('lon'), may hold values from -0.375 to 0.375
- lat_factor: bfloat16 [128, 384], P('lat'), may hold values from -0.75 to 0.75
Outputs:
- core: float32 [96, 192, 384], P(('grp', 'lev'), 'lon', 'lat'), parts along dimension 0
There are 2 independent parts, one for each index of `grp`. A program takes and returns all parts, laid end to end along the dimension named above; an argument that names none is the same for every part. Nothing has to cross between parts.
All inputs are finite; a program needn't handle non-finite values.
Results may differ from a plain program's by a relative error of at most 0.0003.
Values may be sent and summed in bfloat16 or wider, within the bound.
A program may use at most 64 MiB of HBM per device.

v0:
```python
import jax
import jax.numpy as jnp
from jax import lax
from jax.sharding import PartitionSpec as P


def body(snapshot, level_factor, lon_factor, lat_factor):
    first = lax.psum_scatter(
        jnp.einsum("kij,kr->rij", snapshot, level_factor, preferred_element_type=jnp.float32),
        "lev",
        scatter_dimension=0,
        tiled=True,
    )
    lon_term = jnp.einsum(
        "rij,js->ris", first, lon_factor.astype(jnp.float32), precision=lax.Precision.HIGHEST
    )
    second = lax.psum_scatter(lon_term, "lon", scatter_dimension=2, tiled=True)
    lat_term = jnp.einsum(
        "ris,it->rst", second, lat_factor.astype(jnp.float32), precision=lax.Precision.HIGHEST
    )
    return lax.psum_scatter(lat_term, "lat", scatter_dimension=2, tiled=True)


def solution(mesh):
    in_specs = (P(("grp", "lev"), "lat", "lon"), P("lev", None), P("lon", None), P("lat", None))
    out_specs = P(("grp", "lev"), "lon", "lat")
    return jax.shard_map(body, mesh=mesh, in_specs=in_specs, out_specs=out_specs, check_vma=False)
```

profile of v0, /device:TPU:0, one launch (start us, length us, event | category | flops | bytes accessed | tf_op | source)
XLA Modules:
  0.0 137.9 jit_solution(13263286483788428691)
XLA Ops:
  6.5 0.0 copy-start
  6.5 0.0 reduce-scatter.8.cloned.1.call-start
  6.5 1.2 copy-done
  7.8 1.6 %fusion.2 = f32[48,32,256]{2,0,1:T(8,128)S(1)} fusion(bf16[64,32,256]{2,1,0:T(8,128)(2,1)S(1)} %copy-done, bf16[64,48]{0,1:T(8,128)(2,1)} %param.5), kind=kOutput, calls=%fused_computation.2 | convolution fusion | flops 50331648 | bytes 2627584 | tf_op jit(solution)/shard_map/kij,kr->rij/dot_general | solution.py:9
  9.3 2.1 %copy.6 = f32[48,32,256]{2,1,0:T(8,128)} copy(f32[48,32,256]{2,0,1:T(8,128)S(1)} %fusion.2) | data formatting | bytes 3145728 | tf_op jit(solution)/shard_map/kij,kr->rij/dot_general | solution.py:9
  11.4 0.0 copy-start.1
  11.4 0.0 reduce-scatter.8.cloned.1.call-update
  11.4 0.0 reduce-scatter.10.cloned.1.call-start
  11.5 11.9 %reduce-scatter.8.cloned.1.call-done = f32[24,32,256]{2,1,0:T(8,128)} async-done(((f32[48,32,256]{2,1,0:T(8,128)}), f32[24,32,256]{2,1,0:T(8,128)}) %reduce-scatter.8.cloned.1.call-update) | async-done | bytes 786448 | tf_op jit(solution)/shard_map/reduce_scatter | solution.py:8
  23.3 0.0 copy-done.1
  23.3 2.5 %fusion.4 = f32[24,32,192]{2,1,0:T(8,128)} fusion(f32[24,32,256]{2,1,0:T(8,128)} %reduce-scatter.8.cloned.1.call-done, bf16[256,192]{0,1:T(8,128)(2,1)S(1)} %copy-done.1), kind=kOutput, calls=%fused_computation.4 | convolution fusion | flops 452984832 | bytes 1474560 | tf_op jit(solution)/shard_map/rij,js->ris/dot_general | solution.py:14
  25.9 2.0 %copy.7 = f32[24,32,192]{1,0,2:T(8,128)S(1)} copy(f32[24,32,192]{2,1,0:T(8,128)} %fusion.4) | data formatting | bytes 1179648
  27.8 1.4 %reshape.3 = f32[192,768]{1,0:T(8,128)} reshape(f32[192,24,32]{2,1,0:T(8,128)S(1)} %bitcast.15) | data formatting | bytes 1179648
  29.3 0.0 copy-start.2
  29.3 0.0 reduce-scatter.10.cloned.1.call-update
  29.3 0.0 reduce-scatter.12.cloned.1.call-start
  29.3 16.6 %reduce-scatter.10.cloned.1.call-done = f32[96,768]{1,0:T(8,128)} async-done(((f32[192,768]{1,0:T(8,128)}), f32[96,768]{1,0:T(8,128)}) %reduce-scatter.10.cloned.1.call-update) | async-done | bytes 294928
  45.9 1.3 reshape.4
  47.3 0.0 copy-done.2
  47.3 3.3 %fusion = f32[24,96,384]{2,1,0:T(8,128)} fusion(f32[24,32,96]{1,0,2:T(8,128)S(1)} %bitcast.17, bf16[32,384]{1,0:T(8,128)(2,1)S(1)} %copy-done.2), kind=kOutput, calls=%fused_computation | convolution fusion | flops 339738624 | bytes 3858432 | tf_op jit(solution)/shard_map/ris,it->rst/dot_general | solution.py:18
  50.6 5.5 %copy.9 = f32[24,96,384]{1,0,2:T(8,128)} copy(f32[24,96,384]{2,1,0:T(8,128)} %fusion) | data formatting | bytes 7077888
  56.2 5.3 %reshape.5 = f32[384,2304]{1,0:T(8,128)} reshape(f32[384,24,96]{2,1,0:T(8,128)} %bitcast.14) | data formatting | bytes 7077888
  61.5 0.0 reduce-scatter.12.cloned.1.call-update
  61.5 66.5 %reduce-scatter.12.cloned.1.call-done = f32[96,2304]{1,0:T(8,128)} async-done(((f32[384,2304]{1,0:T(8,128)}), f32[96,2304]{1,0:T(8,128)}) %reduce-scatter.12.cloned.1.call-update) | async-done | bytes 884752
  128.0 2.0 %reshape.6 = f32[96,24,96]{2,1,0:T(8,128)S(1)} reshape(f32[96,2304]{1,0:T(8,128)} %reduce-scatter.12.cloned.1.call-done) | data formatting | bytes 1769472
  130.0 1.4 %copy.10 = f32[24,96,96]{2,1,0:T(8,128)} copy(f32[24,96,96]{1,0,2:T(8,128)S(1)} %bitcast.16) | data formatting | bytes 1769472
Async XLA Ops:
  6.5 1.2 copy-start
  6.5 16.8 %reduce-scatter.8.cloned.1.call-start = ((), (), s32[]{:S(2)}) async-start(), calls=%async_computation.3 | async-start | bytes 2359296 | tf_op jit(solution)/shard_map/reduce_scatter | solution.py:8
  11.4 11.9 %copy-start.1 = (bf16[256,192]{0,1:T(8,128)(2,1)S(1)}, bf16[256,192]{0,1:T(8,128)(2,1)}, u32[]{:S(2)}) copy-start(bf16[256,192]{0,1:T(8,128)(2,1)} %param.6) | copy-start | bytes 294916
  11.4 34.5 %reduce-scatter.10.cloned.1.call-start = ((), (), s32[]{:S(2)}) async-start(), calls=%async_computation.4 | async-start | bytes 884736
  29.3 18.0 %copy-start.2 = (bf16[32,384]{1,0:T(8,128)(2,1)S(1)}, bf16[32,384]{1,0:T(8,128)(2,1)}, u32[]{:S(2)}) copy-start(bf16[32,384]{1,0:T(8,128)(2,1)} %param.7) | copy-start | bytes 73732
  29.3 98.7 %reduce-scatter.12.cloned.1.call-start = ((), (), s32[]{:S(2)}) async-start(), calls=%async_computation.5 | async-start | bytes 4423680
Sparse Core Ops, SparseCore 0:
  11.6 11.7 reduce-scatter.7
  29.4 16.4 reduce-scatter.9
  61.6 66.3 reduce-scatter.11
where the time goes:
time: 138 us
  waiting for transfers between devices  95 us (69%)
  local copies, waits for them, and re-layouts  22.3 us (16%)
  between operations  13.1 us (9%)
  matrix products  7.41 us (5%)
    unnamed x5, waiting for transfers between devices  83.2 us
    unnamed x13, local copies, waits for them, and re-layouts  20.2 us
    reduce_scatter x1, waiting for transfers between devices, body(): lax.psum_scatter(jnp.einsum('kij,kr->rij', snapshot, level_factor, prefer...  11.9 us
    dot_general x1, matrix products, body(): jnp.einsum('ris,it->rst', second, lat_factor.astype(jnp.float32), precisi...  3.33 us
  transfers between devices with their start and end apart: 3, of which 3 were waited for; matrix products, arithmetic and copies ran while one was open for 0% of the time, Pallas kernels for 0%

commit v1 on v0

--- a/solution.py
+++ b/solution.py
@@ -1,7 +1,17 @@
+import functools
+
 import jax
 import jax.numpy as jnp
 from jax import lax
+from jax.experimental import pallas as pl
+from jax.experimental.pallas import tpu as pltpu
 from jax.sharding import PartitionSpec as P
+
+MESH = pl.DeviceIdType.MESH
+F32, BF16 = jnp.float32, jnp.bfloat16
+SCALE = 2.0**13
+RG = 8
+IB = 16
 
 
 def body(snapshot, level_factor, lon_factor, lat_factor):
@@ -21,7 +31,259 @@
     return lax.psum_scatter(lat_term, "lat", scatter_dimension=2, tiled=True)
 
 
+def iota(shape, dim):
+    return lax.broadcasted_iota(jnp.int32, shape, dim)
+
+
+def dot(a, b):
+    return jnp.dot(a, b, preferred_element_type=F32)
+
+
+def dot_nt(a, b):
+    return lax.dot_general(a, b, (((1,), (1,)), ((), ())), preferred_element_type=F32)
+
+
+def encode(v, gain):
+    w = v * gain
+    w2 = w * w
+    w4 = w2 * w2
+    w8 = w4 * w4
+    return jnp.where(w < 0, -w8, w8).astype(BF16)
+
+
+def decode(u, factor):
+    u = u.astype(F32)
+    fourth = lax.rsqrt(lax.rsqrt(jnp.maximum(jnp.abs(u), 1e-37)))
+    root = fourth * lax.rsqrt(fourth) * factor
+    return jnp.where(u < 0, -root, jnp.where(u > 0, root, 0.0))
+
+
+def hi_lo(v):
+    hi = v.astype(BF16)
+    return hi, (v - hi.astype(F32)).astype(BF16)
+
+
+def kernel(
+    nz, x_ref, l_ref, o_ref, a_ref, out_ref,
+    mx, w, f_ref, pown, psend, precv, xs, xr, g, ag, ptile, pr, mt, acc,
+    d_send, d_recv, p_send, p_recv, x_send, x_recv, a_send, a_recv, m_send, m_recv, g_send, g_recv,
+):
+    nk, ni, nj = x_ref.shape
+    nr = l_ref.shape[1]
+    ns = o_ref.shape[1]
+    half = nr // 2
+    nq = half // RG
+    sh = ns // 2
+    nt = a_ref.shape[1]
+    tb = nt // nz
+    lanes = RG * ni
+    z = lax.axis_index("lat")
+    x = lax.axis_index("lon")
+    c = lax.axis_index("lev")
+    mates = ({"lev": 1 - c}, {"lon": 1 - x}, {"lon": 1 - x, "lev": 1 - c})
+    zpeers = [lax.rem(z + d, nz) for d in range(1, nz)]
+
+    barrier = pltpu.get_barrier_semaphore()
+    for mate in mates:
+        pl.semaphore_signal(barrier, inc=1, device_id=mate, device_id_type=MESH)
+    for peer in zpeers:
+        pl.semaphore_signal(barrier, inc=1, device_id={"lat": peer}, device_id_type=MESH)
+
+    def remote(src, dst, ss, rs, dev):
+        return pltpu.make_async_remote_copy(
+            src_ref=src, dst_ref=dst, send_sem=ss, recv_sem=rs, device_id=dev, device_id_type=MESH
+        )
+
+    rows, cols = nr * IB, nk * IB
+    spread_r = (iota((rows, nr), 0) // IB == iota((rows, nr), 1)).astype(BF16)
+    spread_k = (iota((nk, cols), 1) // IB == iota((nk, cols), 0)).astype(BF16)
+    lr = dot_nt(spread_r, l_ref[...]).astype(BF16)
+    same = iota((rows, cols), 0) % IB == iota((rows, cols), 1) % IB
+    mx[...] = jnp.where(same, dot(lr, spread_k), 0.0).astype(BF16)
+
+    pl.semaphore_wait(barrier, 3 + nz - 1)
+    a_copies = [
+        remote(a_ref, ag.at[z], a_send.at[d], a_recv.at[z], {"lat": peer}) for d, peer in enumerate(zpeers)
+    ]
+    for copy in a_copies:
+        copy.start()
+    ag[z] = a_ref[...]
+
+    ot = jnp.transpose(o_ref[...].astype(F32)).astype(BF16)
+    most = jnp.zeros((8, 128), F32)
+    d_copies = []
+    for side in range(2):
+        h = (1 - c) if side == 0 else c
+        rws = pl.ds(pl.multiple_of(h * (half * IB), half * IB), half * IB)
+        part = mx[rws, :]
+        for ib in range(ni // IB):
+            blk = x_ref[:, ib * IB : (ib + 1) * IB, :].reshape(nk * IB, nj)
+            f_ref[:, ib] = dot(part, blk).reshape(half, IB, nj)
+        for q in range(nq):
+            hi, lo = hi_lo(f_ref[q * RG : (q + 1) * RG].reshape(lanes, nj))
+            p = dot_nt(ot, hi) + dot_nt(ot, lo)
+            m = jnp.max(jnp.abs(p).reshape(ns // 8, 8, lanes), axis=0)
+            for j in range(lanes // 128):
+                most = jnp.maximum(most, m[:, j * 128 : (j + 1) * 128])
+            if side == 0:
+                psend[q] = p
+                copy = remote(psend.at[q], precv.at[q], d_send.at[q], d_recv.at[q], mates[0])
+                copy.start()
+                d_copies.append(copy)
+            else:
+                pown[q] = p
+    ptile[...] = most
+    p_copies = [
+        remote(ptile, pr.at[n], p_send.at[n], p_recv.at[n], mate) for n, mate in enumerate(mates)
+    ]
+    for copy in p_copies:
+        copy.start()
+
+    w[...] = jnp.zeros(w.shape, BF16)
+    for d, peer in enumerate(zpeers):
+        remote(a_ref, ag.at[peer], a_send.at[d], a_recv.at[peer], {"lat": peer}).wait_recv()
+    pick = iota((nt, 128), 1)
+    pick = ((iota((nt, 128), 0) == pick + z * tb) & (pick < tb)).astype(BF16)
+    for b in range(nz):
+        mine = dot(ag[b], pick).astype(BF16)
+        for r in range(RG):
+            w[b, r * ni : (r + 1) * ni, r * 128 : (r + 1) * 128] = mine
+    acc[...] = jnp.zeros(acc.shape, F32)
+
+    for copy in p_copies:
+        copy.wait()
+    m = jnp.maximum(jnp.maximum(most, pr[0]), jnp.maximum(pr[1], pr[2]))
+    m = jnp.maximum(jnp.max(jnp.max(m, axis=0, keepdims=True), axis=1, keepdims=True), 1e-30)
+    mt[z] = jnp.broadcast_to(m, (8, 128))
+    m_copies = [
+        remote(mt.at[z], mt.at[z], m_send.at[d], m_recv.at[z], {"lat": peer}) for d, peer in enumerate(zpeers)
+    ]
+    for copy in m_copies:
+        copy.start()
+    gain, factor = SCALE / m, m * (1.0 / SCALE)
+
+    mine = pl.ds(pl.multiple_of(x * sh, sh), sh)
+    theirs = pl.ds(pl.multiple_of((1 - x) * sh, sh), sh)
+    x_copies = []
+    for q in range(nq):
+        d_copies[q].wait_recv()
+        xs[q] = encode(pown[q, theirs, :] + precv[q, theirs, :], gain)
+        copy = remote(xs.at[q], xr.at[q], x_send.at[q], x_recv.at[q], mates[1])
+        copy.start()
+        x_copies.append(copy)
+
+    def hop(side, d, b, q):
+        to = z + 1 if side == 0 else z - 1
+        return remote(g.at[b, q], g.at[b, q], g_send.at[side, d, q], g_recv.at[b, q], {"lat": to})
+
+    def goes(side):
+        return z < nz - 1 if side == 0 else z > 0
+
+    def block(side, d):
+        return z - d if side == 0 else z + d
+
+    def exists(b):
+        return (b >= 0) & (b < nz)
+
+    for q in range(nq):
+        x_copies[q].wait_recv()
+        val = pown[q, mine, :] + precv[q, mine, :] + decode(xr[q], factor)
+        g[z, q] = encode(val, gain)
+        for side in range(2):
+
+            @pl.when(goes(side))
+            def _():
+                hop(side, 0, z, q).start()
+
+    def use(b):
+        lhs = decode(g[b].reshape(nq * sh, lanes), mt[b][0:1, 0:1] * (1.0 / SCALE))
+        hi, lo = hi_lo(lhs)
+        acc[...] += dot(hi, w[b]) + dot(lo, w[b])
+
+    use(z)
+    for d, peer in enumerate(zpeers):
+        remote(mt.at[z], mt.at[peer], m_send.at[d], m_recv.at[peer], {"lat": peer}).wait_recv()
+
+    @pl.loop(1, nz)
+    def _(d):
+        for q in range(nq):
+            for side in range(2):
+                b = block(side, d)
+
+                @pl.when(exists(b))
+                def _():
+                    hop(side, 0, b, q).wait_recv()
+
+                    @pl.when(goes(side))
+                    def _():
+                        hop(side, d, b, q).start()
+
+        @pl.loop(0, 2)
+        def _(side):
+            b = jnp.where(side == 0, z - d, z + d)
+
+            @pl.when(exists(b))
+            def _():
+                use(b)
+
+    for q in range(nq):
+        for r in range(RG):
+            out_ref[q * RG + r] = acc[q * sh : (q + 1) * sh, r * 128 : r * 128 + tb]
+
+    for copy in a_copies + d_copies + m_copies + x_copies:
+        copy.wait_send()
+
+    @pl.loop(0, nz - 1)
+    def _(d):
+        for q in range(nq):
+            for side in range(2):
+                b = block(side, d)
+
+                @pl.when(exists(b) & goes(side))
+                def _():
+                    hop(side, d, b, q).wait_send()
+
+
+def fused(nz, snapshot, level_factor, lon_factor, lat_factor):
+    nk, ni, nj = snapshot.shape
+    nr, ns, nt = level_factor.shape[1], lon_factor.shape[1], lat_factor.shape[1]
+    half, sh, tb, lanes = nr // 2, ns // 2, nt // nz, RG * ni
+    nq = half // RG
+    dma = lambda *shape: pltpu.SemaphoreType.DMA(shape)
+    vmem = pl.BlockSpec(memory_space=pltpu.VMEM)
+    return pl.pallas_call(
+        functools.partial(kernel, nz),
+        out_shape=jax.ShapeDtypeStruct((half, sh, tb), F32),
+        in_specs=[vmem] * 4,
+        out_specs=vmem,
+        scratch_shapes=[
+            pltpu.VMEM((nr * IB, nk * IB), BF16),
+            pltpu.VMEM((nz, lanes, RG * 128), BF16),
+            pltpu.VMEM((half, ni // IB, IB, nj), F32),
+            pltpu.VMEM((nq, ns, lanes), F32),
+            pltpu.VMEM((nq, ns, lanes), F32),
+            pltpu.VMEM((nq, ns, lanes), F32),
+            pltpu.VMEM((nq, sh, lanes), BF16),
+            pltpu.VMEM((nq, sh, lanes), BF16),
+            pltpu.VMEM((nz, nq, sh, lanes), BF16),
+            pltpu.VMEM((nz, ni, nt), BF16),
+            pltpu.VMEM((8, 128), F32),
+            pltpu.VMEM((3, 8, 128), F32),
+            pltpu.VMEM((nz, 8, 128), F32),
+            pltpu.VMEM((nq * sh, RG * 128), F32),
+            dma(nq), dma(nq), dma(3), dma(3), dma(nq), dma(nq),
+            dma(nz - 1), dma(nz), dma(nz - 1), dma(nz), dma(2, nz, nq), dma(nz, nq),
+        ],
+        compiler_params=pltpu.CompilerParams(
+            collective_id=0, has_side_effects=True, vmem_limit_bytes=40 * 2**20
+        ),
+    )(snapshot, level_factor, lon_factor, lat_factor)
+
+
 def solution(mesh):
     in_specs = (P(("grp", "lev"), "lat", "lon"), P("lev", None), P("lon", None), P("lat", None))
     out_specs = P(("grp", "lev"), "lon", "lat")
-    return jax.shard_map(body, mesh=mesh, in_specs=in_specs, out_specs=out_specs, check_vma=False)
+    size = dict(mesh.shape)
+    small = size["lev"] == 2 and size["lon"] == 2 and 1 < size["lat"] <= 4
+    part = functools.partial(fused, size["lat"]) if small else body
+    return jax.shard_map(part, mesh=mesh, in_specs=in_specs, out_specs=out_specs, check_vma=False)

time: 138 us -> 30.8 us (0.22)
  waiting for transfers between devices: 95 us -> 0 us
  Pallas kernels: 0 us -> 25.7 us
  local copies, waits for them, and re-layouts: 22.3 us -> 4.76 us
  between operations: 13.1 us -> 0.03 us
  matrix products: 7.41 us -> 0 us
    unnamed x5 -> x0, waiting for transfers between devices: 83.2 us -> none
    pallas_call x0 -> x1, Pallas kernels: none -> 25.7 us  [fused(): pl.pallas_call(functools.partial(kernel, nz), out_shape=jax.ShapeDtypeStr...]
    unnamed x13 -> x7, local copies, waits for them, and re-layouts: 20.2 us -> 4.76 us
    reduce_scatter x1 -> x0, waiting for transfers between devices: 11.9 us -> none  [body(): lax.psum_scatter(jnp.einsum('kij,kr->rij', snapshot, level_factor, prefer...]
    dot_general x3 -> x0, matrix products: 7.41 us -> none  [the longest x1 3.33 us: body(): jnp.einsum('ris,it->rst', second, lat_factor.astype(jnp.float32), precisi...]
    dot_general x1 -> x0, local copies, waits for them, and re-layouts: 2.09 us -> none  [body(): jnp.einsum('kij,kr->rij', snapshot, level_factor, preferred_element_type=...]
  transfers between devices with their start and end apart: 3 -> 0, of which waited for: 3 -> 0; matrix products, arithmetic and copies ran while one was open for 0% -> 0% of each run, Pallas kernels for 0% -> 0%
where the time goes in v1:
time: 30.8 us; the launch traced here: 30.5 us
  Pallas kernels  25.7 us (83%)
  local copies, waits for them, and re-layouts  4.76 us (15%)
    pallas_call x1, Pallas kernels, fused(): pl.pallas_call(functools.partial(kernel, nz), out_shape=jax.ShapeDtypeStr...  25.7 us
    unnamed x7, local copies, waits for them, and re-layouts  4.76 us

profile of v1, /device:TPU:0, one launch (start us, length us, event | category | flops | bytes accessed | tf_op | source)
XLA Modules:
  0.0 30.5 jit_solution(10060986923133215222)
XLA Ops:
  0.0 0.8 %copy.5.l_ref = bf16[64,48]{1,0:T(8,128)(2,1)S(1)} copy(bf16[64,48]{0,1:T(8,128)(2,1)} %param.5) | data formatting | bytes 12288 | tf_op args[1]
  0.8 1.0 %copy.6.o_ref = bf16[256,192]{1,0:T(8,128)(2,1)S(1)} copy(bf16[256,192]{0,1:T(8,128)(2,1)} %param.6) | data formatting | bytes 196608 | tf_op args[2]
  1.8 0.0 copy-start
  1.8 1.2 %copy-done = bf16[64,32,256]{2,1,0:T(8,128)(2,1)S(1)} copy-done((bf16[64,32,256]{2,1,0:T(8,128)(2,1)S(1)}, bf16[64,32,256]{2,1,0:T(8,128)(2,1)}, u32[]{:S(2)}) %copy-start) | copy-done | bytes 1048600
  3.0 0.0 copy-start.1
  3.0 0.7 %copy-done.1 = bf16[32,384]{1,0:T(8,128)(2,1)S(1)} copy-done((bf16[32,384]{1,0:T(8,128)(2,1)S(1)}, bf16[32,384]{1,0:T(8,128)(2,1)}, u32[]{:S(2)}) %copy-start.1) | copy-done | bytes 24600
  3.8 25.7 %shard_map.46 = f32[24,96,96]{2,1,0:T(8,128)S(1)} custom-call(bf16[64,32,256]{2,1,0:T(8,128)(2,1)S(1)} %copy-done, bf16[64,48]{1,0:T(8,128)(2,1)S(1)} %copy.5.l_ref, bf16[256,192]{1,0:T(8,128)(2,1)S(1)} %copy.6.o_ref, bf16[32,384]{1,0:T(8,128)(2,1)S(1)} %copy-done.1), custom_call_target="tpu_custom_call" | custom-call | tf_op jit(solution)/shard_map/pallas_call | solution.py:254
  29.5 1.0 %copy.8 = f32[24,96,96]{2,1,0:T(8,128)} copy(f32[24,96,96]{2,1,0:T(8,128)S(1)} %shard_map.46) | data formatting | bytes 1769472
Async XLA Ops:
  1.8 1.2 %copy-start = (bf16[64,32,256]{2,1,0:T(8,128)(2,1)S(1)}, bf16[64,32,256]{2,1,0:T(8,128)(2,1)}, u32[]{:S(2)}) copy-start(bf16[64,32,256]{2,1,0:T(8,128)(2,1)} %x_ref.1) | copy-start | bytes 3145732
  3.0 0.7 %copy-start.1 = (bf16[32,384]{1,0:T(8,128)(2,1)S(1)}, bf16[32,384]{1,0:T(8,128)(2,1)}, u32[]{:S(2)}) copy-start(bf16[32,384]{1,0:T(8,128)(2,1)} %a_ref.1) | copy-start | bytes 73732

commit v2 on v1

--- a/solution.py
+++ b/solution.py
@@ -9,7 +9,8 @@
 
 MESH = pl.DeviceIdType.MESH
 F32, BF16 = jnp.float32, jnp.bfloat16
-SCALE = 2.0**13
+TOP = 2.0**7
+KNEE = 2.0**-6
 RG = 8
 IB = 16
 
@@ -45,17 +46,21 @@
 
 def encode(v, gain):
     w = v * gain
+    small = jnp.abs(w) < KNEE
     w2 = w * w
     w4 = w2 * w2
     w8 = w4 * w4
-    return jnp.where(w < 0, -w8, w8).astype(BF16)
+    w16 = w8 * w8
+    return jnp.where(small, w * (KNEE**15), jnp.where(w < 0, -w16, w16)).astype(BF16)
 
 
 def decode(u, factor):
     u = u.astype(F32)
-    fourth = lax.rsqrt(lax.rsqrt(jnp.maximum(jnp.abs(u), 1e-37)))
-    root = fourth * lax.rsqrt(fourth) * factor
-    return jnp.where(u < 0, -root, jnp.where(u > 0, root, 0.0))
+    size = jnp.abs(u)
+    root = jnp.maximum(size, KNEE**16)
+    root = lax.rsqrt(lax.rsqrt(root))
+    root = lax.rsqrt(lax.rsqrt(root))
+    return jnp.where(size < KNEE**16, u * (KNEE**-15), jnp.where(u < 0, -root, root)) * factor
 
 
 def hi_lo(v):
@@ -64,17 +69,17 @@
 
 
 def kernel(
-    nz, x_ref, l_ref, o_ref, a_ref, out_ref,
-    mx, w, f_ref, pown, psend, precv, xs, xr, g, ag, ptile, pr, mt, acc,
+    nz, x_hbm, l_hbm, o_hbm, a_hbm, out_ref,
+    x_ref, l_ref, o_ref, in_sem, mx, w, f_ref, pown, psend, precv, xs, xr, g, ag, ptile, pr, mt, acc,
     d_send, d_recv, p_send, p_recv, x_send, x_recv, a_send, a_recv, m_send, m_recv, g_send, g_recv,
 ):
     nk, ni, nj = x_ref.shape
-    nr = l_ref.shape[1]
-    ns = o_ref.shape[1]
+    nr = l_ref.shape[0]
+    ns = o_ref.shape[0]
     half = nr // 2
     nq = half // RG
     sh = ns // 2
-    nt = a_ref.shape[1]
+    nt = a_hbm.shape[1]
     tb = nt // nz
     lanes = RG * ni
     z = lax.axis_index("lat")
@@ -83,6 +88,12 @@
     mates = ({"lev": 1 - c}, {"lon": 1 - x}, {"lon": 1 - x, "lev": 1 - c})
     zpeers = [lax.rem(z + d, nz) for d in range(1, nz)]
 
+    loads = [
+        pltpu.make_async_copy(src, dst, in_sem.at[n])
+        for n, (src, dst) in enumerate(((l_hbm, l_ref), (a_hbm, ag.at[z]), (x_hbm, x_ref), (o_hbm, o_ref)))
+    ]
+    for load in loads:
+        load.start()
     barrier = pltpu.get_barrier_semaphore()
     for mate in mates:
         pl.semaphore_signal(barrier, inc=1, device_id=mate, device_id_type=MESH)
@@ -97,19 +108,22 @@
     rows, cols = nr * IB, nk * IB
     spread_r = (iota((rows, nr), 0) // IB == iota((rows, nr), 1)).astype(BF16)
     spread_k = (iota((nk, cols), 1) // IB == iota((nk, cols), 0)).astype(BF16)
-    lr = dot_nt(spread_r, l_ref[...]).astype(BF16)
-    same = iota((rows, cols), 0) % IB == iota((rows, cols), 1) % IB
-    mx[...] = jnp.where(same, dot(lr, spread_k), 0.0).astype(BF16)
-
+    same = (iota((IB, 128), 0) == iota((IB, 128), 1) % IB).astype(F32)
+    loads[0].wait()
+    lr = dot(spread_r, l_ref[...]).astype(BF16)
+    for j in range(cols // 128):
+        spread = dot(lr, spread_k[:, j * 128 : (j + 1) * 128]).reshape(nr, IB, 128) * same
+        mx[:, j * 128 : (j + 1) * 128] = spread.reshape(rows, 128).astype(BF16)
+
+    loads[1].wait()
     pl.semaphore_wait(barrier, 3 + nz - 1)
     a_copies = [
-        remote(a_ref, ag.at[z], a_send.at[d], a_recv.at[z], {"lat": peer}) for d, peer in enumerate(zpeers)
+        remote(ag.at[z], ag.at[z], a_send.at[d], a_recv.at[z], {"lat": peer}) for d, peer in enumerate(zpeers)
     ]
     for copy in a_copies:
         copy.start()
-    ag[z] = a_ref[...]
-
-    ot = jnp.transpose(o_ref[...].astype(F32)).astype(BF16)
+    loads[2].wait()
+    loads[3].wait()
     most = jnp.zeros((8, 128), F32)
     d_copies = []
     for side in range(2):
@@ -121,7 +135,7 @@
             f_ref[:, ib] = dot(part, blk).reshape(half, IB, nj)
         for q in range(nq):
             hi, lo = hi_lo(f_ref[q * RG : (q + 1) * RG].reshape(lanes, nj))
-            p = dot_nt(ot, hi) + dot_nt(ot, lo)
+            p = dot_nt(o_ref[...], hi) + dot_nt(o_ref[...], lo)
             m = jnp.max(jnp.abs(p).reshape(ns // 8, 8, lanes), axis=0)
             for j in range(lanes // 128):
                 most = jnp.maximum(most, m[:, j * 128 : (j + 1) * 128])
@@ -141,7 +155,7 @@
 
     w[...] = jnp.zeros(w.shape, BF16)
     for d, peer in enumerate(zpeers):
-        remote(a_ref, ag.at[peer], a_send.at[d], a_recv.at[peer], {"lat": peer}).wait_recv()
+        remote(ag.at[z], ag.at[peer], a_send.at[d], a_recv.at[peer], {"lat": peer}).wait_recv()
     pick = iota((nt, 128), 1)
     pick = ((iota((nt, 128), 0) == pick + z * tb) & (pick < tb)).astype(BF16)
     for b in range(nz):
@@ -160,7 +174,7 @@
     ]
     for copy in m_copies:
         copy.start()
-    gain, factor = SCALE / m, m * (1.0 / SCALE)
+    gain, factor = (TOP / 4) / m, m * (4 / TOP)
 
     mine = pl.ds(pl.multiple_of(x * sh, sh), sh)
     theirs = pl.ds(pl.multiple_of((1 - x) * sh, sh), sh)
@@ -195,12 +209,13 @@
             def _():
                 hop(side, 0, z, q).start()
 
-    def use(b):
-        lhs = decode(g[b].reshape(nq * sh, lanes), mt[b][0:1, 0:1] * (1.0 / SCALE))
-        hi, lo = hi_lo(lhs)
-        acc[...] += dot(hi, w[b]) + dot(lo, w[b])
-
-    use(z)
+    def use(b, q):
+        hi, lo = hi_lo(decode(g[b, q], mt[b][0:1, 0:1] * (4 / TOP)))
+        both = dot(jnp.concatenate([hi, lo], axis=0), w[b])
+        acc[q] += both[:sh] + both[sh:]
+
+    for q in range(nq):
+        use(z, q)
     for d, peer in enumerate(zpeers):
         remote(mt.at[z], mt.at[peer], m_send.at[d], m_recv.at[peer], {"lat": peer}).wait_recv()
 
@@ -218,17 +233,18 @@
                     def _():
                         hop(side, d, b, q).start()
 
-        @pl.loop(0, 2)
-        def _(side):
-            b = jnp.where(side == 0, z - d, z + d)
-
-            @pl.when(exists(b))
-            def _():
-                use(b)
+        @pl.loop(0, nq)
+        def _(q):
+            for side in range(2):
+                b = block(side, d)
+
+                @pl.when(exists(b))
+                def _():
+                    use(b, q)
 
     for q in range(nq):
         for r in range(RG):
-            out_ref[q * RG + r] = acc[q * sh : (q + 1) * sh, r * 128 : r * 128 + tb]
+            out_ref[q * RG + r] = acc[q, :, r * 128 : r * 128 + tb]
 
     for copy in a_copies + d_copies + m_copies + x_copies:
         copy.wait_send()
@@ -254,9 +270,13 @@
     return pl.pallas_call(
         functools.partial(kernel, nz),
         out_shape=jax.ShapeDtypeStruct((half, sh, tb), F32),
-        in_specs=[vmem] * 4,
+        in_specs=[pl.BlockSpec(memory_space=pltpu.HBM)] * 4,
         out_specs=vmem,
         scratch_shapes=[
+            pltpu.VMEM((nk, ni, nj), BF16),
+            pltpu.VMEM((nr, nk), BF16),
+            pltpu.VMEM((ns, nj), BF16),
+            dma(4),
             pltpu.VMEM((nr * IB, nk * IB), BF16),
             pltpu.VMEM((nz, lanes, RG * 128), BF16),
             pltpu.VMEM((half, ni // IB, IB, nj), F32),
@@ -270,14 +290,14 @@
             pltpu.VMEM((8, 128), F32),
             pltpu.VMEM((3, 8, 128), F32),
             pltpu.VMEM((nz, 8, 128), F32),
-            pltpu.VMEM((nq * sh, RG * 128), F32),
+            pltpu.VMEM((nq, sh, RG * 128), F32),
             dma(nq), dma(nq), dma(3), dma(3), dma(nq), dma(nq),
             dma(nz - 1), dma(nz), dma(nz - 1), dma(nz), dma(2, nz, nq), dma(nz, nq),
         ],
         compiler_params=pltpu.CompilerParams(
-            collective_id=0, has_side_effects=True, vmem_limit_bytes=40 * 2**20
+            collective_id=0, has_side_effects=True, vmem_limit_bytes=63 * 2**20
         ),
-    )(snapshot, level_factor, lon_factor, lat_factor)
+    )(snapshot, level_factor.T, lon_factor.T, lat_factor)
 
 
 def solution(mesh):

time: 30.8 us -> 30.1 us (0.977)
  local copies, waits for them, and re-layouts: 4.76 us -> 2.36 us
  Pallas kernels: 25.7 us -> 27.5 us
    unnamed x7 -> x1, local copies, waits for them, and re-layouts: 4.76 us -> 2.36 us
    pallas_call x1, Pallas kernels: 25.7 us -> 27.5 us  [fused(): pl.pallas_call(functools.partial(kernel, nz), out_shape=jax.ShapeDtypeStr...]
where the time goes in v2:
time: 30.1 us; the launch traced here: 29.9 us
  Pallas kernels  27.5 us (91%)
  local copies, waits for them, and re-layouts  2.36 us (8%)
    pallas_call x1, Pallas kernels, fused(): pl.pallas_call(functools.partial(kernel, nz), out_shape=jax.ShapeDtypeStr...  27.5 us
    unnamed x1, local copies, waits for them, and re-layouts  2.36 us

profile of v2, /device:TPU:0, one launch (start us, length us, event | category | flops | bytes accessed | tf_op | source)
XLA Modules:
  0.0 29.9 jit_solution(12219978127649661028)
XLA Ops:
  0.0 27.5 %shard_map.46 = f32[24,96,96]{2,1,0:T(8,128)} custom-call(bf16[64,32,256]{2,1,0:T(8,128)(2,1)} %x_hbm.1, bf16[48,64]{1,0:T(8,128)(2,1)} %bitcast.3, bf16[192,256]{1,0:T(8,128)(2,1)} %bitcast.2, bf16[32,384]{1,0:T(8,128)(2,1)} %a_hbm.1), custom_call_target="tpu_custom_call" | custom-call | tf_op jit(solution)/shard_map/pallas_call | solution.py:270
  27.5 2.4 %copy.6 = f32[24,96,96]{2,1,0:T(8,128)} copy(f32[24,96,96]{2,1,0:T(8,128)} %shard_map.46) | data formatting | bytes 1769472

commit v3 on v2

--- a/solution.py
+++ b/solution.py
@@ -85,7 +85,7 @@
     z = lax.axis_index("lat")
     x = lax.axis_index("lon")
     c = lax.axis_index("lev")
-    mates = ({"lev": 1 - c}, {"lon": 1 - x}, {"lon": 1 - x, "lev": 1 - c})
+    mates = ({"lev": 1 - c}, {"lon": 1 - x})
     zpeers = [lax.rem(z + d, nz) for d in range(1, nz)]
 
     loads = [
@@ -116,7 +116,7 @@
         mx[:, j * 128 : (j + 1) * 128] = spread.reshape(rows, 128).astype(BF16)
 
     loads[1].wait()
-    pl.semaphore_wait(barrier, 3 + nz - 1)
+    pl.semaphore_wait(barrier, 2 + nz - 1)
     a_copies = [
         remote(ag.at[z], ag.at[z], a_send.at[d], a_recv.at[z], {"lat": peer}) for d, peer in enumerate(zpeers)
     ]
@@ -124,7 +124,6 @@
         copy.start()
     loads[2].wait()
     loads[3].wait()
-    most = jnp.zeros((8, 128), F32)
     d_copies = []
     for side in range(2):
         h = (1 - c) if side == 0 else c
@@ -136,9 +135,6 @@
         for q in range(nq):
             hi, lo = hi_lo(f_ref[q * RG : (q + 1) * RG].reshape(lanes, nj))
             p = dot_nt(o_ref[...], hi) + dot_nt(o_ref[...], lo)
-            m = jnp.max(jnp.abs(p).reshape(ns // 8, 8, lanes), axis=0)
-            for j in range(lanes // 128):
-                most = jnp.maximum(most, m[:, j * 128 : (j + 1) * 128])
             if side == 0:
                 psend[q] = p
                 copy = remote(psend.at[q], precv.at[q], d_send.at[q], d_recv.at[q], mates[0])
@@ -146,12 +142,27 @@
                 d_copies.append(copy)
             else:
                 pown[q] = p
-    ptile[...] = most
-    p_copies = [
-        remote(ptile, pr.at[n], p_send.at[n], p_recv.at[n], mate) for n, mate in enumerate(mates)
-    ]
-    for copy in p_copies:
+    most = jnp.zeros((8, 128), F32)
+    for q in range(nq):
+        d_copies[q].wait_recv()
+        pown[q] = pown[q] + precv[q]
+        m = jnp.max(jnp.abs(pown[q]).reshape(ns // 8, 8, lanes), axis=0)
+        for j in range(lanes // 128):
+            most = jnp.maximum(most, m[:, j * 128 : (j + 1) * 128])
+    m_own = jnp.max(jnp.max(most, axis=0, keepdims=True), axis=1, keepdims=True)
+    m_own = jnp.maximum(m_own, 1e-30)
+    gain = TOP / m_own
+    ptile[...] = jnp.broadcast_to(m_own, (8, 128))
+    p_copy = remote(ptile, pr, p_send, p_recv, mates[1])
+    p_copy.start()
+    mine = pl.ds(pl.multiple_of(x * sh, sh), sh)
+    theirs = pl.ds(pl.multiple_of((1 - x) * sh, sh), sh)
+    x_copies = []
+    for q in range(nq):
+        xs[q] = encode(pown[q, theirs, :], gain)
+        copy = remote(xs.at[q], xr.at[q], x_send.at[q], x_recv.at[q], mates[1])
         copy.start()
+        x_copies.append(copy)
 
     w[...] = jnp.zeros(w.shape, BF16)
     for d, peer in enumerate(zpeers):
@@ -159,32 +170,20 @@
     pick = iota((nt, 128), 1)
     pick = ((iota((nt, 128), 0) == pick + z * tb) & (pick < tb)).astype(BF16)
     for b in range(nz):
-        mine = dot(ag[b], pick).astype(BF16)
+        own_t = dot(ag[b], pick).astype(BF16)
         for r in range(RG):
-            w[b, r * ni : (r + 1) * ni, r * 128 : (r + 1) * 128] = mine
-    acc[...] = jnp.zeros(acc.shape, F32)
-
-    for copy in p_copies:
-        copy.wait()
-    m = jnp.maximum(jnp.maximum(most, pr[0]), jnp.maximum(pr[1], pr[2]))
-    m = jnp.maximum(jnp.max(jnp.max(m, axis=0, keepdims=True), axis=1, keepdims=True), 1e-30)
+            w[b, r * ni : (r + 1) * ni, r * 128 : (r + 1) * 128] = own_t
+
+    p_copy.wait()
+    m_x = pr[0:1, 0:1]
+    m = m_own + m_x
     mt[z] = jnp.broadcast_to(m, (8, 128))
     m_copies = [
         remote(mt.at[z], mt.at[z], m_send.at[d], m_recv.at[z], {"lat": peer}) for d, peer in enumerate(zpeers)
     ]
     for copy in m_copies:
         copy.start()
-    gain, factor = (TOP / 4) / m, m * (4 / TOP)
-
-    mine = pl.ds(pl.multiple_of(x * sh, sh), sh)
-    theirs = pl.ds(pl.multiple_of((1 - x) * sh, sh), sh)
-    x_copies = []
-    for q in range(nq):
-        d_copies[q].wait_recv()
-        xs[q] = encode(pown[q, theirs, :] + precv[q, theirs, :], gain)
-        copy = remote(xs.at[q], xr.at[q], x_send.at[q], x_recv.at[q], mates[1])
-        copy.start()
-        x_copies.append(copy)
+    gain, factor = TOP / m, m_x * (1 / TOP)
 
     def hop(side, d, b, q):
         to = z + 1 if side == 0 else z - 1
@@ -201,7 +200,7 @@
 
     for q in range(nq):
         x_copies[q].wait_recv()
-        val = pown[q, mine, :] + precv[q, mine, :] + decode(xr[q], factor)
+        val = pown[q, mine, :] + decode(xr[q], factor)
         g[z, q] = encode(val, gain)
         for side in range(2):
 
@@ -209,13 +208,13 @@
             def _():
                 hop(side, 0, z, q).start()
 
-    def use(b, q):
-        hi, lo = hi_lo(decode(g[b, q], mt[b][0:1, 0:1] * (4 / TOP)))
+    def use(b, q, own=False):
+        hi, lo = hi_lo(decode(g[b, q], mt[b][0:1, 0:1] * (1 / TOP)))
         both = dot(jnp.concatenate([hi, lo], axis=0), w[b])
-        acc[q] += both[:sh] + both[sh:]
-
-    for q in range(nq):
-        use(z, q)
+        acc[q] = both[:sh] + both[sh:] + (0.0 if own else acc[q])
+
+    for q in range(nq):
+        use(z, q, own=True)
     for d, peer in enumerate(zpeers):
         remote(mt.at[z], mt.at[peer], m_send.at[d], m_recv.at[peer], {"lat": peer}).wait_recv()
 
@@ -269,7 +268,7 @@
     vmem = pl.BlockSpec(memory_space=pltpu.VMEM)
     return pl.pallas_call(
         functools.partial(kernel, nz),
-        out_shape=jax.ShapeDtypeStruct((half, sh, tb), F32),
+        out_shape=pltpu.VMEM((half, sh, tb), F32),
         in_specs=[pl.BlockSpec(memory_space=pltpu.HBM)] * 4,
         out_specs=vmem,
         scratch_shapes=[
@@ -288,14 +287,14 @@
             pltpu.VMEM((nz, nq, sh, lanes), BF16),
             pltpu.VMEM((nz, ni, nt), BF16),
             pltpu.VMEM((8, 128), F32),
-            pltpu.VMEM((3, 8, 128), F32),
+            pltpu.VMEM((8, 128), F32),
             pltpu.VMEM((nz, 8, 128), F32),
             pltpu.VMEM((nq, sh, RG * 128), F32),
-            dma(nq), dma(nq), dma(3), dma(3), dma(nq), dma(nq),
+            dma(nq), dma(nq), pltpu.SemaphoreType.DMA, pltpu.SemaphoreType.DMA, dma(nq), dma(nq),
             dma(nz - 1), dma(nz), dma(nz - 1), dma(nz), dma(2, nz, nq), dma(nz, nq),
         ],
         compiler_params=pltpu.CompilerParams(
-            collective_id=0, has_side_effects=True, vmem_limit_bytes=63 * 2**20
+            collective_id=0, has_side_effects=True, vmem_limit_bytes=58 * 2**20
         ),
     )(snapshot, level_factor.T, lon_factor.T, lat_factor)
 

time: 30.1 us -> 26.5 us (0.88)
  Pallas kernels: 27.5 us -> 25.2 us
  local copies, waits for them, and re-layouts: 2.36 us -> 1.02 us
    pallas_call x1, Pallas kernels: 27.5 us -> 25.2 us  [fused(): pl.pallas_call(functools.partial(kernel, nz), out_shape=pltpu.VMEM((half,...]
    unnamed x1, local copies, waits for them, and re-layouts: 2.36 us -> 1.02 us
where the time goes in v3:
time: 26.5 us; the launch traced here: 26.3 us
  Pallas kernels  25.2 us (95%)
  local copies, waits for them, and re-layouts  1.02 us (4%)
    pallas_call x1, Pallas kernels, fused(): pl.pallas_call(functools.partial(kernel, nz), out_shape=pltpu.VMEM((half,...  25.2 us
    unnamed x1, local copies, waits for them, and re-layouts  1.02 us

profile of v3, /device:TPU:0, one launch (start us, length us, event | category | flops | bytes accessed | tf_op | source)
XLA Modules:
  0.0 26.3 jit_solution(1861433074819322563)
XLA Ops:
  0.0 25.2 %shard_map.46 = f32[24,96,96]{2,1,0:T(8,128)S(1)} custom-call(bf16[64,32,256]{2,1,0:T(8,128)(2,1)} %x_hbm.1, bf16[48,64]{1,0:T(8,128)(2,1)} %bitcast.3, bf16[192,256]{1,0:T(8,128)(2,1)} %bitcast.2, bf16[32,384]{1,0:T(8,128)(2,1)} %a_hbm.1), custom_call_target="tpu_custom_call" | custom-call | tf_op jit(solution)/shard_map/pallas_call | solution.py:269
  25.3 1.0 %copy.6 = f32[24,96,96]{2,1,0:T(8,128)} copy(f32[24,96,96]{2,1,0:T(8,128)S(1)} %shard_map.46) | data formatting | bytes 1769472

commit v4 on v3

--- a/solution.py
+++ b/solution.py
@@ -185,28 +185,36 @@
         copy.start()
     gain, factor = TOP / m, m_x * (1 / TOP)
 
-    def hop(side, d, b, q):
-        to = z + 1 if side == 0 else z - 1
-        return remote(g.at[b, q], g.at[b, q], g_send.at[side, d, q], g_recv.at[b, q], {"lat": to})
-
-    def goes(side):
-        return z < nz - 1 if side == 0 else z > 0
-
-    def block(side, d):
-        return z - d if side == 0 else z + d
+    def away(side, d):
+        return z + d if side == 0 else z - d
 
     def exists(b):
         return (b >= 0) & (b < nz)
+
+    def send(side, d, q):
+        to = away(side, d)
+        return remote(g.at[z, q], g.at[z, q], g_send.at[side, d - 1, q], g_recv.at[z, q], {"lat": to})
+
+    def forward(side, q):
+        b, to = away(1 - side, 2), away(side, 1)
+        return remote(g.at[b, q], g.at[b, q], g_send.at[side, 2, q], g_recv.at[b, q], {"lat": to})
+
+    def forwards(side):
+        return exists(away(1 - side, 2)) & exists(away(side, 1))
+
+    def arrival(b, q):
+        return remote(g.at[z, q], g.at[b, q], g_send.at[0, 0, q], g_recv.at[b, q], {"lat": zpeers[0]})
 
     for q in range(nq):
         x_copies[q].wait_recv()
         val = pown[q, mine, :] + decode(xr[q], factor)
         g[z, q] = encode(val, gain)
-        for side in range(2):
-
-            @pl.when(goes(side))
-            def _():
-                hop(side, 0, z, q).start()
+        for d in (2, 1):
+            for side in range(2):
+
+                @pl.when(exists(away(side, d)))
+                def _():
+                    send(side, d, q).start()
 
     def use(b, q, own=False):
         hi, lo = hi_lo(decode(g[b, q], mt[b][0:1, 0:1] * (1 / TOP)))
@@ -218,27 +226,28 @@
     for d, peer in enumerate(zpeers):
         remote(mt.at[z], mt.at[peer], m_send.at[d], m_recv.at[peer], {"lat": peer}).wait_recv()
 
-    @pl.loop(1, nz)
-    def _(d):
-        for q in range(nq):
-            for side in range(2):
-                b = block(side, d)
-
-                @pl.when(exists(b))
+    for q in range(nq):
+        for side in range(2):
+
+            @pl.when(exists(away(1 - side, 2)))
+            def _():
+                arrival(away(1 - side, 2), q).wait_recv()
+
+                @pl.when(forwards(side))
                 def _():
-                    hop(side, 0, b, q).wait_recv()
-
-                    @pl.when(goes(side))
-                    def _():
-                        hop(side, d, b, q).start()
+                    forward(side, q).start()
+
+    for d in range(1, nz):
 
         @pl.loop(0, nq)
         def _(q):
             for side in range(2):
-                b = block(side, d)
+                b = away(side, d)
 
                 @pl.when(exists(b))
                 def _():
+                    if d != 2:
+                        arrival(b, q).wait_recv()
                     use(b, q)
 
     for q in range(nq):
@@ -248,15 +257,17 @@
     for copy in a_copies + d_copies + m_copies + x_copies:
         copy.wait_send()
 
-    @pl.loop(0, nz - 1)
-    def _(d):
-        for q in range(nq):
-            for side in range(2):
-                b = block(side, d)
-
-                @pl.when(exists(b) & goes(side))
+    for q in range(nq):
+        for side in range(2):
+            for d in (1, 2):
+
+                @pl.when(exists(away(side, d)))
                 def _():
-                    hop(side, d, b, q).wait_send()
+                    send(side, d, q).wait_send()
+
+            @pl.when(forwards(side))
+            def _():
+                forward(side, q).wait_send()
 
 
 def fused(nz, snapshot, level_factor, lon_factor, lat_factor):
@@ -291,7 +302,7 @@
             pltpu.VMEM((nz, 8, 128), F32),
             pltpu.VMEM((nq, sh, RG * 128), F32),
             dma(nq), dma(nq), pltpu.SemaphoreType.DMA, pltpu.SemaphoreType.DMA, dma(nq), dma(nq),
-            dma(nz - 1), dma(nz), dma(nz - 1), dma(nz), dma(2, nz, nq), dma(nz, nq),
+            dma(nz - 1), dma(nz), dma(nz - 1), dma(nz), dma(2, 3, nq), dma(nz, nq),
         ],
         compiler_params=pltpu.CompilerParams(
             collective_id=0, has_side_effects=True, vmem_limit_bytes=58 * 2**20

time: 26.5 us -> 26.8 us (1.011)
  Pallas kernels: 25.2 us -> 25.6 us
    pallas_call x1, Pallas kernels: 25.2 us -> 25.6 us  [fused(): pl.pallas_call(functools.partial(kernel, nz), out_shape=pltpu.VMEM((half,...]
where the time goes in v4:
time: 26.8 us; the launch traced here: 26.6 us
  Pallas kernels  25.6 us (96%)
  local copies, waits for them, and re-layouts  1.02 us (4%)
    pallas_call x1, Pallas kernels, fused(): pl.pallas_call(functools.partial(kernel, nz), out_shape=pltpu.VMEM((half,...  25.6 us
    unnamed x1, local copies, waits for them, and re-layouts  1.02 us

profile of v4, /device:TPU:0, one launch (start us, length us, event | category | flops | bytes accessed | tf_op | source)
XLA Modules:
  0.0 26.6 jit_solution(4281833447330949290)
XLA Ops:
  0.0 25.6 %shard_map.46 = f32[24,96,96]{2,1,0:T(8,128)S(1)} custom-call(bf16[64,32,256]{2,1,0:T(8,128)(2,1)} %x_hbm.1, bf16[48,64]{1,0:T(8,128)(2,1)} %bitcast.3, bf16[192,256]{1,0:T(8,128)(2,1)} %bitcast.2, bf16[32,384]{1,0:T(8,128)(2,1)} %a_hbm.1), custom_call_target="tpu_custom_call" | custom-call | tf_op jit(solution)/shard_map/pallas_call | solution.py:280
  25.6 1.0 %copy.6 = f32[24,96,96]{2,1,0:T(8,128)} copy(f32[24,96,96]{2,1,0:T(8,128)S(1)} %shard_map.46) | data formatting | bytes 1769472

commit v5 on v4

--- a/solution.py
+++ b/solution.py
@@ -237,7 +237,22 @@
                 def _():
                     forward(side, q).start()
 
-    for d in range(1, nz):
+        for side in range(2):
+            b = away(side, 1)
+
+            @pl.when(exists(b))
+            def _():
+                arrival(b, q).wait_recv()
+                use(b, q)
+
+        for side in range(2):
+            b = away(side, 2)
+
+            @pl.when(exists(b))
+            def _():
+                use(b, q)
+
+    for d in range(3, nz):
 
         @pl.loop(0, nq)
         def _(q):
@@ -246,8 +261,7 @@
 
                 @pl.when(exists(b))
                 def _():
-                    if d != 2:
-                        arrival(b, q).wait_recv()
+                    arrival(b, q).wait_recv()
                     use(b, q)
 
     for q in range(nq):

time: 26.8 us -> 26.9 us (level)
  no operation moved by 1% of the time
where the time goes in v5:
time: 26.9 us; the launch traced here: 26.7 us
  Pallas kernels  25.7 us (96%)
  local copies, waits for them, and re-layouts  1.02 us (4%)
    pallas_call x1, Pallas kernels, fused(): pl.pallas_call(functools.partial(kernel, nz), out_shape=pltpu.VMEM((half,...  25.7 us
    unnamed x1, local copies, waits for them, and re-layouts  1.02 us

profile of v5, /device:TPU:0, one launch (start us, length us, event | category | flops | bytes accessed | tf_op | source)
XLA Modules:
  0.0 26.7 jit_solution(14850121559365641325)
XLA Ops:
  0.0 25.7 %shard_map.46 = f32[24,96,96]{2,1,0:T(8,128)S(1)} custom-call(bf16[64,32,256]{2,1,0:T(8,128)(2,1)} %x_hbm.1, bf16[48,64]{1,0:T(8,128)(2,1)} %bitcast.3, bf16[192,256]{1,0:T(8,128)(2,1)} %bitcast.2, bf16[32,384]{1,0:T(8,128)(2,1)} %a_hbm.1), custom_call_target="tpu_custom_call" | custom-call | tf_op jit(solution)/shard_map/pallas_call | solution.py:294
  25.7 1.0 %copy.6 = f32[24,96,96]{2,1,0:T(8,128)} copy(f32[24,96,96]{2,1,0:T(8,128)S(1)} %shard_map.46) | data formatting | bytes 1769472
